TPU v7x, 32 devices: a whole 2x2x4 slice. The times are simulated.
32 devices in a mesh: groups: 2 (over y), ctx: 4 (over z), dp: 2 (over x), mp: 2 (over core).
Axes of the slice: x: 2, y: 2, z: 4, core: 2. Of those that a mesh axis runs over, the one named last changes fastest.
Arguments:
- byte_ids: int32 [4, 1024], P(('groups', 'dp'), 'ctx'), parts along dimension 0, may hold values from 0 to 255
- lengths: int32 [4], P(('groups', 'dp')), parts along dimension 0, may hold values from 128 to 1024, as said below
- hidden: bfloat16 [4, 256, 768], P(('groups', 'dp'), 'ctx'), parts along dimension 0
- w_qkv: bfloat16 [768, 3, 768], P(None, None, 'mp'), may hold values from -0.21875 to 0.21875
- w_out: bfloat16 [768, 768], P('mp'), may hold values from -0.21875 to 0.21875
- w_up: bfloat16 [4, 768, 768], P(None, None, 'mp'), may hold values from -0.109375 to 0.109375
- w_head: bfloat16 [768, 256], P('mp'), may hold values from -0.21875 to 0.21875
Outputs:
- grad_hidden: bfloat16 [4, 256, 768], P(('groups', 'dp'), 'ctx'), parts along dimension 0
There are 2 independent parts, one for each index of `groups`. A program takes and returns all parts, laid end to end along the dimension named above; an argument that names none is the same for every part. Nothing has to cross between parts.
Inputs may be any that keep to these rules, and one draw needn't show every extreme that they name: `lengths`: each document's valid byte count; in every draw some document is full, with 1024 valid bytes.
All inputs are finite; a program needn't handle non-finite values.
Results may differ from a plain program's by a relative error of at most 0.025.
Values may be sent and summed in bfloat16 or wider, within the bound.
A program may use at most 64 MiB of HBM per device.

v0:
```python
import jax
import jax.numpy as jnp
from jax import lax
from jax.sharding import PartitionSpec as P

HEAD_DIM = 64


def with_halo(x, sides, width):
    for axis, dim in sides:
        devices, length = (lax.axis_size(axis), x.shape[dim])
        up = [(i, (i + 1) % devices) for i in range(devices - 1)]
        down = [(j, i) for i, j in up]
        last = lax.slice_in_dim(x, length - width, length, axis=dim)
        initial = lax.slice_in_dim(x, 0, width, axis=dim)
        before = lax.ppermute(last, axis, up)
        after = lax.ppermute(initial, axis, down)
        x = jnp.concatenate([before, x, after], axis=dim)
    return x


def pair_sum(values):
    return lax.psum(values, "mp")


def edges(values):
    return with_halo(values, (("ctx", 0),), 1)


def gelu_grad(pre_act, incoming):
    result, pullback = jax.vjp(jax.nn.gelu, pre_act)
    return pullback(incoming)[0]


def body(byte_ids, lengths, hidden, w_qkv, w_out, w_up, w_head):
    inputs = hidden[0]
    rows = inputs.shape[0]
    model_width = inputs.shape[1]
    split_width = w_qkv.shape[2]
    own_heads = split_width // HEAD_DIM
    scaling = HEAD_DIM ** (-0.5)
    length = lengths[0]
    my_first = lax.axis_index("ctx") * rows
    byte_rows = 4 * rows
    flat_qkv = w_qkv.reshape(model_width, 3 * split_width)
    projected = jnp.dot(inputs, flat_qkv, preferred_element_type=jnp.float32).astype(jnp.bfloat16)
    projected = projected.reshape(rows, 3, own_heads, HEAD_DIM)
    queries = projected[:, 0]
    key_rows = projected[:, 1]
    value_rows = projected[:, 2]

    def usable(first_row, count):
        return 4 * (first_row + jnp.arange(count, dtype=jnp.int32)) < length

    running = jnp.full((rows, own_heads), -1e30, jnp.float32)
    key_piece = lax.all_gather(key_rows, "ctx", axis=0, tiled=True)
    value_piece = lax.all_gather(value_rows, "ctx", axis=0, tiled=True)
    keep = usable(jnp.int32(0), key_piece.shape[0])[None, None, :]
    scores = (
        jnp.einsum("qhd,khd->qhk", queries, key_piece, preferred_element_type=jnp.float32) * scaling
    )
    newest = jnp.maximum(running, jnp.max(jnp.where(keep, scores, -1e30), axis=-1))
    weights = jnp.where(keep, jnp.exp(scores - newest[..., None]), 0.0)
    totals = jnp.sum(weights, axis=-1)
    weighted = jnp.einsum(
        "qhk,khd->qhd",
        weights.astype(jnp.bfloat16),
        value_piece,
        preferred_element_type=jnp.float32,
    )
    weighted, running, totals = (weighted, newest, totals)
    attn_heads = (weighted / totals[..., None]).astype(jnp.bfloat16)
    attn = attn_heads.reshape(rows, split_width)
    log_norm = running + jnp.log(totals)
    context = (
        inputs.astype(jnp.float32)
        + pair_sum(jnp.dot(attn, w_out, preferred_element_type=jnp.float32))
    ).astype(jnp.bfloat16)
    extended = edges(context)
    tap_outputs = [
        jnp.dot(extended, w_up[tap], preferred_element_type=jnp.float32) for tap in range(4)
    ]
    phases = []
    for phase in range(4):
        phase_sum = jnp.zeros((rows, split_width), jnp.float32)
        for tap in range(4):
            shifted = 1 + (phase + tap - 1) // 4
            phase_sum = phase_sum + tap_outputs[tap][shifted : shifted + rows]
        phases.append(phase_sum)
    pre_act = jnp.stack(phases, axis=1).reshape(byte_rows, split_width)
    activated = jax.nn.gelu(pre_act).astype(jnp.bfloat16)
    logits = pair_sum(jnp.dot(activated, w_head, preferred_element_type=jnp.float32))
    byte_first = lax.axis_index("ctx") * byte_rows
    byte_mask = byte_first + jnp.arange(byte_rows, dtype=jnp.int32) < length
    inverse = 1.0 / length.astype(jnp.float32)
    softmaxed = jax.nn.softmax(logits, axis=-1)
    onehot = (byte_ids[0][:, None] == jnp.arange(logits.shape[1], dtype=jnp.int32)[None, :]).astype(
        jnp.float32
    )
    logit_grad = ((softmaxed - onehot) * jnp.where(byte_mask, inverse, 0.0)[:, None]).astype(
        jnp.bfloat16
    )
    act_grad = jnp.dot(logit_grad, w_head.T, preferred_element_type=jnp.float32)
    pre_grad = gelu_grad(pre_act, act_grad).astype(jnp.bfloat16)
    grad_ext = edges(pre_grad.reshape(rows, 4 * split_width)).reshape(byte_rows + 8, split_width)
    partial_grad = jnp.zeros((rows, model_width), jnp.float32)
    for offset in range(4):
        window = grad_ext[5 - offset : 5 - offset + byte_rows].astype(jnp.float32)
        tap_sum = jnp.sum(window.reshape(rows, 4, split_width), axis=1).astype(jnp.bfloat16)
        partial_grad = partial_grad + jnp.dot(
            tap_sum, w_up[offset].T, preferred_element_type=jnp.float32
        )
    context_grad = pair_sum(partial_grad)
    attn_grad = jnp.dot(
        context_grad.astype(jnp.bfloat16), w_out.T, preferred_element_type=jnp.float32
    ).astype(jnp.bfloat16)
    attn_grad = attn_grad.reshape(rows, own_heads, HEAD_DIM)
    row_dots = jnp.sum(attn_grad.astype(jnp.float32) * attn_heads.astype(jnp.float32), axis=-1)
    key_piece = lax.all_gather(key_rows, "ctx", axis=0, tiled=True)
    value_piece = lax.all_gather(value_rows, "ctx", axis=0, tiled=True)
    keep = usable(jnp.int32(0), key_piece.shape[0])[None, None, :]
    scores = (
        jnp.einsum("qhd,khd->qhk", queries, key_piece, preferred_element_type=jnp.float32) * scaling
    )
    probs = jnp.where(keep, jnp.exp(scores - log_norm[..., None]), 0.0)
    product = jnp.einsum("qhd,khd->qhk", attn_grad, value_piece, preferred_element_type=jnp.float32)
    score_grad = (probs * (product - row_dots[..., None])).astype(jnp.bfloat16)
    query_sum = jnp.einsum(
        "qhk,khd->qhd", score_grad, key_piece, preferred_element_type=jnp.float32
    )
    query_grad = (query_sum * scaling).astype(jnp.bfloat16)
    key_keep = usable(my_first, rows)[None, None, :]
    norm_all, dots_all = (
        lax.all_gather(log_norm, "ctx", axis=0, tiled=True),
        lax.all_gather(row_dots, "ctx", axis=0, tiled=True),
    )
    query_piece = lax.all_gather(queries, "ctx", axis=0, tiled=True)
    outgrad_piece = lax.all_gather(attn_grad, "ctx", axis=0, tiled=True)
    count = query_piece.shape[0]
    scores = (
        jnp.einsum("qhd,khd->qhk", query_piece, key_rows, preferred_element_type=jnp.float32)
        * scaling
    )
    probs = jnp.where(key_keep, jnp.exp(scores - norm_all[..., None]), 0.0)
    product = jnp.einsum(
        "qhd,khd->qhk", outgrad_piece, value_rows, preferred_element_type=jnp.float32
    )
    score_grad = (probs * (product - dots_all[..., None])).astype(jnp.bfloat16)
    key_sum = jnp.einsum(
        "qhk,qhd->khd", score_grad, query_piece, preferred_element_type=jnp.float32
    )
    value_sum = jnp.einsum(
        "qhk,qhd->khd",
        probs.astype(jnp.bfloat16),
        outgrad_piece,
        preferred_element_type=jnp.float32,
    )
    key_sum, value_sum = (key_sum, value_sum)
    key_grad = (key_sum * scaling).astype(jnp.bfloat16)
    value_grad = value_sum.astype(jnp.bfloat16)
    stacked = jnp.stack([query_grad, key_grad, value_grad], axis=1).reshape(rows, 3 * split_width)
    back_proj = pair_sum(jnp.dot(stacked, flat_qkv.T, preferred_element_type=jnp.float32))
    input_grad = (context_grad + back_proj).astype(jnp.bfloat16)
    return input_grad[None]


def solution(mesh):
    placed = (
        P(("groups", "dp"), "ctx"),
        P(("groups", "dp")),
        P(("groups", "dp"), "ctx", None),
        P(None, None, "mp"),
        P("mp", None),
        P(None, None, "mp"),
        P("mp", None),
    )
    return jax.shard_map(
        body,
        mesh=mesh,
        in_specs=placed,
        out_specs=P(("groups", "dp"), "ctx", None),
        check_vma=False,
    )
```

profile of v0, /device:TPU:0, one launch (start us, length us, event | category | flops | bytes accessed | tf_op | source)
XLA Modules:
  0.0 255.1 jit_solution(12642925866357019696)
XLA Ops:
  7.3 2.6 %copy.24 = bf16[768,3,384]{0,2,1:T(8,128)(2,1)S(1)} copy(bf16[768,3,384]{2,0,1:T(8,128)(2,1)} %param.10) | data formatting | bytes 3538944 | tf_op args[3]
  12.2 17.3 %all-gather.1 = bf16[256,1,6,64]{3,2,1,0:T(8,128)(2,1)S(1)} all-gather(bf16[64,1,6,64]{3,2,1,0:T(8,128)(2,1)S(1)} %get-tuple-element.11), channel_id=3, replica_groups=mesh['groups'=2,'ctx'=4,'dp'=2,'mp'=2] {'ctx'}, dimensions={0}, use_global_device_ids=true | all-gather | bytes 245760 | tf_op jit(solution)/shard_map/all_gather | solution.py:56
  32.7 16.3 %all-gather = bf16[256,1,6,64]{3,2,1,0:T(8,128)(2,1)S(1)} all-gather(bf16[64,1,6,64]{3,2,1,0:T(8,128)(2,1)S(1)} %get-tuple-element.9), channel_id=2, replica_groups=mesh['groups'=2,'ctx'=4,'dp'=2,'mp'=2] {'ctx'}, dimensions={0}, use_global_device_ids=true | all-gather | bytes 245760 | tf_op jit(solution)/shard_map/all_gather | solution.py:57
  52.5 18.5 %all-reduce.5.cloned.1.call-done = f32[64,768]{1,0:T(8,128)} async-done(((f32[64,768]{1,0:T(8,128)}), f32[64,768]{1,0:T(8,128)}) %all-reduce.5.cloned.1.call-update) | async-done | bytes 196624 | tf_op jit(solution)/shard_map/psum | solution.py:23
  72.0 3.6 %collective-permute-start = (bf16[1,768]{1,0:T(2,128)(2,1)S(1)}, bf16[1,768]{1,0:T(2,128)(2,1)S(1)}, u32[]{:S(2)}, u32[]{:S(2)}) collective-permute-start(bf16[1,768]{1,0:T(2,128)(2,1)S(1)} %get-tuple-element.17), channel_id=1, source_target_pairs={{0,4},{4,8},{8,12},{1,5},{5,9},{9,13},{2,6},{6,10},{10,14},{3,7},{... | collective-permute-start | bytes 4616 | tf_op jit(solution)/shard_map/ppermute | solution.py:16
  77.0 4.2 %collective-permute-done.1 = bf16[1,768]{1,0:T(2,128)(2,1)S(1)} collective-permute-done((bf16[1,768]{1,0:T(2,128)(2,1)S(1)}, bf16[1,768]{1,0:T(2,128)(2,1)S(1)}, u32[]{:S(2)}, u32[]{:S(2)}) %collective-permute-start.1) | collective-permute-done | bytes 1568 | tf_op jit(solution)/shard_map/ppermute | solution.py:17
  87.6 2.0 fusion.67
  90.2 17.8 %all-reduce.7.cloned.1.call-done = f32[256,256]{1,0:T(8,128)} async-done(((f32[256,256]{1,0:T(8,128)}), f32[256,256]{1,0:T(8,128)}) %all-reduce.7.cloned.1.call-update) | async-done | bytes 262160 | tf_op jit(solution)/shard_map/psum | solution.py:23
  110.2 1.6 fusion.45
  111.9 4.2 %collective-permute-start.2 = (bf16[1,1536]{1,0:T(2,128)(2,1)S(1)}, bf16[1,1536]{1,0:T(2,128)(2,1)}, u32[]{:S(2)}, u32[]{:S(2)}) collective-permute-start(bf16[1,1536]{1,0:T(2,128)(2,1)S(1)} %bitcast.170), channel_id=1, source_target_pairs={{0,4},{4,8},{8,12},{1,5},{5,9},{9,13},{2,6},{6,10},{10,14},{3,7},{... | collective-permute-start | bytes 9224 | tf_op jit(solution)/shard_map/ppermute | solution.py:16
  118.0 15.7 %all-gather.2 = bf16[256,1,6,64]{3,0,2,1:T(8,128)(2,1)S(1)} all-gather(bf16[64,1,6,64]{3,0,2,1:T(8,128)(2,1)S(1)} %copy.46), channel_id=4, replica_groups=mesh['groups'=2,'ctx'=4,'dp'=2,'mp'=2] {'ctx'}, dimensions={0}, use_global_device_ids=true | all-gather | bytes 245760 | tf_op jit(solution)/shard_map/all_gather | solution.py:137
  133.7 13.4 %all-gather.3 = f32[4,64,6]{1,2,0:T(8,128)S(1)} all-gather(f32[1,64,6]{1,2,0:T(8,128)S(1)} %bitcast.168), channel_id=1, replica_groups=mesh['groups'=2,'ctx'=4,'dp'=2,'mp'=2] {'ctx'}, dimensions={0}, use_global_device_ids=true | all-gather | bytes 7680 | tf_op jit(solution)/shard_map/all_gather | solution.py:134
  148.1 1.8 reduce_sum.69
  155.1 2.1 fusion.27
  162.2 2.1 convolution_add_fusion
  165.5 18.4 %all-reduce.9.cloned.1.call-done = f32[64,768]{1,0:T(8,128)} async-done(((f32[64,768]{1,0:T(8,128)}), f32[64,768]{1,0:T(8,128)}) %all-reduce.9.cloned.1.call-update) | async-done | bytes 196624 | tf_op jit(solution)/shard_map/psum | solution.py:23
  183.9 1.9 convolution_convert_fusion.2
  185.7 1.5 copy.33
  188.2 1.7 copy.37
  189.9 2.1 fusion.16
  192.0 13.4 %all-gather.4 = f32[4,64,6]{1,2,0:T(8,128)S(1)} all-gather(f32[1,64,6]{1,2,0:T(8,128)S(1)} %bitcast.169), channel_id=1, replica_groups=mesh['groups'=2,'ctx'=4,'dp'=2,'mp'=2] {'ctx'}, dimensions={0}, use_global_device_ids=true | all-gather | bytes 7680 | tf_op jit(solution)/shard_map/all_gather | solution.py:135
  205.5 17.8 %all_gather.24 = bf16[256,6,64]{2,1,0:T(8,128)(2,1)} all-gather(bf16[64,6,64]{2,1,0:T(8,128)(2,1)} %copy.37), channel_id=1, replica_groups=mesh['groups'=2,'ctx'=4,'dp'=2,'mp'=2] {'ctx'}, dimensions={0}, use_global_device_ids=true | all-gather | bytes 245760 | tf_op jit(solution)/shard_map/all_gather | solution.py:138
  228.9 18.0 %all-reduce.11.cloned.1.call-done = f32[64,768]{1,0:T(8,128)} async-done(((f32[64,768]{1,0:T(8,128)}), f32[64,768]{1,0:T(8,128)}) %all-reduce.11.cloned.1.call-update) | async-done | bytes 196624 | tf_op jit(solution)/shard_map/psum | solution.py:23
  246.9 1.7 fusion.75
  (86 shorter events, 41.1 us)
Async XLA Ops:
  6.5 44.9 %copy-start = (bf16[384,768]{1,0:T(8,128)(2,1)S(1)}, bf16[384,768]{1,0:T(8,128)(2,1)}, u32[]{:S(2)}) copy-start(bf16[384,768]{1,0:T(8,128)(2,1)} %param.11) | copy-start | bytes 1769476
  6.5 3.4 %copy-start.3 = (bf16[1,64,768]{2,1,0:T(8,128)(2,1)S(1)}, bf16[1,64,768]{2,1,0:T(8,128)(2,1)}, u32[]{:S(2)}) copy-start(bf16[1,64,768]{2,1,0:T(8,128)(2,1)} %param.9) | copy-start | bytes 294916
  6.5 64.5 %all-reduce.5.cloned.1.call-start = ((), (), s32[]{:S(2)}) async-start(), calls=%async_computation | async-start | bytes 393216 | tf_op jit(solution)/shard_map/psum | solution.py:23
  7.3 42.9 %copy-start.8 = (pred[256]{0:T(512)(128)(4,1)}, pred[256]{0:T(512)(128)(4,1)S(1)}, u32[]{:S(2)}) copy-start(pred[256]{0:T(512)(128)(4,1)S(1)} %multiply_compare_fusion) | copy-start | bytes 772
  11.6 0.7 copy-start.2
  11.6 39.8 %copy-start.1 = (bf16[64,1,6,64]{3,2,1,0:T(8,128)(2,1)}, bf16[64,1,6,64]{3,2,1,0:T(8,128)(2,1)S(1)}, u32[]{:S(2)}) copy-start(bf16[64,1,6,64]{3,2,1,0:T(8,128)(2,1)S(1)} %get-tuple-element.9) | copy-start | bytes 147460
  49.9 21.1 %copy-start.4 = (bf16[1,64,768]{2,1,0:T(8,128)(2,1)S(1)}, bf16[1,64,768]{2,1,0:T(8,128)(2,1)}, u32[]{:S(2)}) copy-start(bf16[1,64,768]{2,1,0:T(8,128)(2,1)} %param.9) | copy-start | bytes 294916
  51.4 35.0 %copy-start.5 = (bf16[64,6,64]{0,2,1:T(8,128)(2,1)}, bf16[64,6,64]{0,2,1:T(8,128)(2,1)S(1)}, u32[]{:S(2)}) copy-start(bf16[64,6,64]{0,2,1:T(8,128)(2,1)S(1)} %fusion.12) | copy-start | bytes 147460
  52.4 55.6 %all-reduce.7.cloned.1.call-start = ((), (), s32[]{:S(2)}) async-start(), calls=%async_computation.1 | async-start | bytes 524288 | tf_op jit(solution)/shard_map/psum | solution.py:23
  72.0 5.0 %collective-permute-start = (bf16[1,768]{1,0:T(2,128)(2,1)S(1)}, bf16[1,768]{1,0:T(2,128)(2,1)S(1)}, u32[]{:S(2)}, u32[]{:S(2)}) collective-permute-start(bf16[1,768]{1,0:T(2,128)(2,1)S(1)} %get-tuple-element.17), channel_id=1, source_target_pairs={{0,4},{4,8},{8,12},{1,5},{5,9},{9,13},{2,6},{6,10},{10,14},{3,7},{... | collective-permute-start | bytes 4616 | tf_op jit(solution)/shard_map/ppermute | solution.py:16
  75.6 5.5 %collective-permute-start.1 = (bf16[1,768]{1,0:T(2,128)(2,1)S(1)}, bf16[1,768]{1,0:T(2,128)(2,1)S(1)}, u32[]{:S(2)}, u32[]{:S(2)}) collective-permute-start(bf16[1,768]{1,0:T(2,128)(2,1)S(1)} %get-tuple-element.18), channel_id=1, source_target_pairs={{4,0},{8,4},{12,8},{5,1},{9,5},{13,9},{6,2},{10,6},{14,10},{7,3},{... | collective-permute-start | bytes 4616 | tf_op jit(solution)/shard_map/ppermute | solution.py:17
  86.4 23.8 %copy-start.9 = (s32[1,256]{1,0:T(1,128)S(1)}, s32[1,256]{1,0:T(1,128)}, u32[]{:S(2)}) copy-start(s32[1,256]{1,0:T(1,128)} %param.7) | copy-start | bytes 3076
  89.6 94.2 %all-reduce.9.cloned.1.call-start = ((), (), s32[]{:S(2)}) async-start(), calls=%async_computation.2 | async-start | bytes 393216 | tf_op jit(solution)/shard_map/psum | solution.py:23
  90.2 43.5 %copy-start.6 = (f32[64,6]{0,1:T(8,128)}, f32[64,6]{0,1:T(8,128)S(1)}, u32[]{:S(2)}) copy-start(f32[64,6]{0,1:T(8,128)S(1)} %log_add_fusion) | copy-start | bytes 4612
  111.9 37.9 %collective-permute-start.2 = (bf16[1,1536]{1,0:T(2,128)(2,1)S(1)}, bf16[1,1536]{1,0:T(2,128)(2,1)}, u32[]{:S(2)}, u32[]{:S(2)}) collective-permute-start(bf16[1,1536]{1,0:T(2,128)(2,1)S(1)} %bitcast.170), channel_id=1, source_target_pairs={{0,4},{4,8},{8,12},{1,5},{5,9},{9,13},{2,6},{6,10},{10,14},{3,7},{... | collective-permute-start | bytes 9224 | tf_op jit(solution)/shard_map/ppermute | solution.py:16
  116.8 33.1 %collective-permute-start.3 = (bf16[1,1536]{1,0:T(2,128)(2,1)}, bf16[1,1536]{1,0:T(2,128)(2,1)}, u32[]{:S(2)}, u32[]{:S(2)}) collective-permute-start(bf16[1,1536]{1,0:T(2,128)(2,1)} %bitcast.43), channel_id=1, source_target_pairs={{4,0},{8,4},{12,8},{5,1},{9,5},{13,9},{6,2},{10,6},{14,10},{7,3},{... | collective-permute-start | bytes 9224 | tf_op jit(solution)/shard_map/ppermute | solution.py:17
  160.7 29.2 %copy-start.7 = (f32[64,6]{0,1:T(8,128)S(1)}, f32[64,6]{0,1:T(8,128)}, u32[]{:S(2)}) copy-start(f32[64,6]{0,1:T(8,128)} %copy-done.6) | copy-start | bytes 4612
  164.2 82.7 %all-reduce.11.cloned.1.call-start = ((), (), s32[]{:S(2)}) async-start(), calls=%async_computation.3 | async-start | bytes 393216 | tf_op jit(solution)/shard_map/psum | solution.py:23
Sparse Core Ops, SparseCore 0:
  52.5 18.4 all-reduce.4
  89.8 18.2 all-reduce.6
  164.4 19.4 all-reduce.8
  229.0 17.8 all-reduce.10
where the time goes:
time: 256 us; the launch traced here: 255 us
  blocking collectives  93.9 us (37%)
  waiting for transfers between devices  77 us (30%)
  matrix products  28.3 us (11%)
  local copies, waits for them, and re-layouts  18.3 us (7%)
  between operations  14.2 us (6%)
  other arithmetic  12.9 us (5%)
  starting transfers between devices  10.6 us (4%)
    psum x4, waiting for transfers between devices, pair_sum(): return lax.psum(values, 'mp')  72.7 us
    all_gather x1, blocking collectives, body(): outgrad_piece = lax.all_gather(attn_grad, 'ctx', axis=0, tiled=True)  17.8 us
    all_gather x1, blocking collectives, body(): key_piece = lax.all_gather(key_rows, 'ctx', axis=0, tiled=True)  17.3 us
    all_gather x1, blocking collectives, body(): value_piece = lax.all_gather(value_rows, 'ctx', axis=0, tiled=True)  16.3 us
    all_gather x1, blocking collectives, body(): query_piece = lax.all_gather(queries, 'ctx', axis=0, tiled=True)  15.7 us
    all_gather x1, blocking collectives, body(): lax.all_gather(row_dots, 'ctx', axis=0, tiled=True)  13.4 us
    all_gather x1, blocking collectives, body(): lax.all_gather(log_norm, 'ctx', axis=0, tiled=True)  13.4 us
    ppermute x2, starting transfers between devices, with_halo(): before = lax.ppermute(last, axis, up)  7.88 us
  transfers between devices with their start and end apart: 8, of which 5 were waited for; matrix products, arithmetic and copies ran while one was open for 2% of the time, Pallas kernels for 0%

commit v1 on v0

--- a/solution.py
+++ b/solution.py
@@ -20,7 +20,7 @@
 
 
 def pair_sum(values):
-    return lax.psum(values, "mp")
+    return jnp.sum(lax.all_gather(values, "mp"), axis=0)
 
 
 def edges(values):

time: 256 us -> 167 us (0.65)
  waiting for transfers between devices: 77 us -> 0.61 us
  between operations: 14.2 us -> 1.2 us
  blocking collectives: 93.9 us -> 103 us
  matrix products: 28.3 us -> 24.3 us
    psum x4 -> x0, waiting for transfers between devices: 72.7 us -> none  [pair_sum(): return lax.psum(values, 'mp')]
    all_gather x0 -> x4, blocking collectives: none -> 8.58 us  [pair_sum(): return jnp.sum(lax.all_gather(values, 'mp'), axis=0)]
    ppermute x2, waiting for transfers between devices: 4.16 us -> 0.6 us  [with_halo(): after = lax.ppermute(initial, axis, down)]
  transfers between devices with their start and end apart: 8 -> 4, of which waited for: 5 -> 1; matrix products, arithmetic and copies ran while one was open for 2% -> 3% of each run, Pallas kernels for 0% -> 0%
where the time goes in v1:
time: 167 us; the launch traced here: 166 us
  blocking collectives  103 us (62%)
  matrix products  24.3 us (15%)
  local copies, waits for them, and re-layouts  16.9 us (10%)
  other arithmetic  10.9 us (7%)
  starting transfers between devices  9.19 us (6%)
    all_gather x1, blocking collectives, body(): outgrad_piece = lax.all_gather(attn_grad, 'ctx', axis=0, tiled=True)  18.3 us
    all_gather x1, blocking collectives, body(): key_piece = lax.all_gather(key_rows, 'ctx', axis=0, tiled=True)  17.3 us
    all_gather x1, blocking collectives, body(): value_piece = lax.all_gather(value_rows, 'ctx', axis=0, tiled=True)  16.3 us
    all_gather x1, blocking collectives, body(): query_piece = lax.all_gather(queries, 'ctx', axis=0, tiled=True)  15.7 us
    all_gather x1, blocking collectives, body(): lax.all_gather(log_norm, 'ctx', axis=0, tiled=True)  13.4 us
    all_gather x1, blocking collectives, body(): lax.all_gather(row_dots, 'ctx', axis=0, tiled=True)  13.1 us
    all_gather x4, blocking collectives, pair_sum(): return jnp.sum(lax.all_gather(values, 'mp'), axis=0)  8.58 us
    ppermute x2, starting transfers between devices, with_halo(): before = lax.ppermute(last, axis, up)  6.61 us
  transfers between devices with their start and end apart: 4, of which 1 were waited for; matrix products, arithmetic and copies ran while one was open for 3% of the time, Pallas kernels for 0%

profile of v1, /device:TPU:0, one launch (start us, length us, event | category | flops | bytes accessed | tf_op | source)
XLA Modules:
  0.0 165.9 jit_solution(6742160512597225645)
XLA Ops:
  0.7 2.6 %copy.42 = bf16[768,3,384]{0,2,1:T(8,128)(2,1)S(1)} copy(bf16[768,3,384]{2,0,1:T(8,128)(2,1)} %param.10) | data formatting | bytes 3538944 | tf_op args[3]
  5.7 17.3 %all-gather.1 = bf16[256,1,6,64]{3,2,1,0:T(8,128)(2,1)S(1)} all-gather(bf16[64,1,6,64]{3,2,1,0:T(8,128)(2,1)S(1)} %get-tuple-element.11), channel_id=3, replica_groups=mesh['groups'=2,'ctx'=4,'dp'=2,'mp'=2] {'ctx'}, dimensions={0}, use_global_device_ids=true | all-gather | bytes 245760 | tf_op jit(solution)/shard_map/all_gather | solution.py:56
  26.1 16.3 %all-gather = bf16[256,1,6,64]{3,2,1,0:T(8,128)(2,1)S(1)} all-gather(bf16[64,1,6,64]{3,2,1,0:T(8,128)(2,1)S(1)} %get-tuple-element.9), channel_id=2, replica_groups=mesh['groups'=2,'ctx'=4,'dp'=2,'mp'=2] {'ctx'}, dimensions={0}, use_global_device_ids=true | all-gather | bytes 245760 | tf_op jit(solution)/shard_map/all_gather | solution.py:57
  45.1 2.1 %all-gather.2 = f32[128,768]{1,0:T(8,128)S(1)} all-gather(f32[64,768]{1,0:T(8,128)S(1)} %fusion.103), channel_id=4, replica_groups=mesh['groups'=2,'ctx'=4,'dp'=2,'mp'=2] {'mp'}, dimensions={0}, use_global_device_ids=true | all-gather | bytes 589824 | tf_op jit(solution)/shard_map/all_gather | solution.py:23
  48.2 2.7 %collective-permute-start = (bf16[1,768]{1,0:T(2,128)(2,1)S(1)}, bf16[1,768]{1,0:T(2,128)(2,1)S(1)}, u32[]{:S(2)}, u32[]{:S(2)}) collective-permute-start(bf16[1,768]{1,0:T(2,128)(2,1)S(1)} %get-tuple-element.17), channel_id=1, source_target_pairs={{0,4},{4,8},{8,12},{1,5},{5,9},{9,13},{2,6},{6,10},{10,14},{3,7},{... | collective-permute-start | bytes 4616 | tf_op jit(solution)/shard_map/ppermute | solution.py:16
  52.2 15.7 %all-gather.5 = bf16[256,1,6,64]{3,0,2,1:T(8,128)(2,1)S(1)} all-gather(bf16[64,1,6,64]{3,0,2,1:T(8,128)(2,1)S(1)} %copy.64), channel_id=7, replica_groups=mesh['groups'=2,'ctx'=4,'dp'=2,'mp'=2] {'ctx'}, dimensions={0}, use_global_device_ids=true | all-gather | bytes 245760 | tf_op jit(solution)/shard_map/all_gather | solution.py:137
  69.0 13.4 %all-gather.7 = f32[4,64,6]{1,2,0:T(8,128)S(1)} all-gather(f32[1,64,6]{1,2,0:T(8,128)S(1)} %bitcast.176), channel_id=1, replica_groups=mesh['groups'=2,'ctx'=4,'dp'=2,'mp'=2] {'ctx'}, dimensions={0}, use_global_device_ids=true | all-gather | bytes 7680 | tf_op jit(solution)/shard_map/all_gather | solution.py:134
  83.8 1.3 fusion.19
  86.4 1.3 fusion.85
  90.2 2.2 %all-gather.3 = f32[512,256]{1,0:T(8,128)S(1)} all-gather(f32[256,256]{1,0:T(8,128)S(1)} %fusion.67), channel_id=5, replica_groups=mesh['groups'=2,'ctx'=4,'dp'=2,'mp'=2] {'mp'}, dimensions={0}, use_global_device_ids=true | all-gather | bytes 786432 | tf_op jit(solution)/shard_map/all_gather | solution.py:23
  92.7 1.6 fusion.45
  94.3 3.9 %collective-permute-start.2 = (bf16[1,1536]{1,0:T(2,128)(2,1)S(1)}, bf16[1,1536]{1,0:T(2,128)(2,1)S(1)}, u32[]{:S(2)}, u32[]{:S(2)}) collective-permute-start(bf16[1,1536]{1,0:T(2,128)(2,1)S(1)} %bitcast.178), channel_id=1, source_target_pairs={{0,4},{4,8},{8,12},{1,5},{5,9},{9,13},{2,6},{6,10},{10,14},{3,7},{... | collective-permute-start | bytes 9224 | tf_op jit(solution)/shard_map/ppermute | solution.py:16
  101.4 1.8 %reduce_sum.107 = bf16[64,384]{1,0:T(8,128)(2,1)} reduce(bf16[64,4,384]{2,1,0:T(4,128)(2,1)} %slice.107, bf16[]{:T(256)} %constant.15.clone.1), dimensions={1}, to_apply=%region_7.8 | reduce | flops 73728 | bytes 245762 | tf_op jit(solution)/shard_map/reduce_sum | solution.py:109
  103.8 1.7 %pad_maximum_fusion.2 = bf16[66,1536]{1,0:T(8,128)(2,1)} fusion(bf16[1,1536]{1,0:T(2,128)(2,1)S(1)} %collective-permute-done.3, bf16[64,1536]{1,0:T(8,128)(2,1)} %reshape.101, bf16[1,1536]{1,0:T(2,128)(2,1)S(1)} %collective-permute-done.2), kind=kLoop, calls=%fused_computation.77 | loop fusion | flops 608256 | bytes 405504 | tf_op jit(solution)/shard_map/concatenate | solution.py:18
  109.2 2.1 %fusion.27 = f32[64,768]{1,0:T(8,128)} fusion(bf16[64,384]{1,0:T(8,128)(2,1)} %reduce.1, bf16[4,768,384]{2,1,0:T(8,128)(2,1)} %param.12), kind=kOutput, calls=%fused_computation.40 | convolution fusion | flops 37748736 | bytes 835584 | tf_op jit(solution)/shard_map/dot_general | solution.py:110
  113.5 1.4 convolution_add_fusion.2
  114.9 1.4 convolution_add_fusion.1
  116.4 1.4 convolution_add_fusion
  117.8 2.2 %all-gather.4 = f32[128,768]{1,0:T(8,128)} all-gather(f32[64,768]{1,0:T(8,128)S(1)} %convolution_add_fusion), channel_id=6, replica_groups=mesh['groups'=2,'ctx'=4,'dp'=2,'mp'=2] {'mp'}, dimensions={0}, use_global_device_ids=true | all-gather | bytes 589824 | tf_op jit(solution)/shard_map/all_gather | solution.py:23
  123.7 2.3 %fusion.16 = bf16[64,1,6,64]{0,3,2,1:T(8,128)(2,1)} fusion(bf16[64,6,64]{0,2,1:T(8,128)(2,1)S(1)} %bitcast.174, f32[64,6,256]{2,0,1:T(8,128)} %copy-done.1, bf16[256,1,6,64]{0,3,2,1:T(8,128)(2,1)} %copy.48, bf16[256,1,6,64]{0,3,2,1:T(8,128)(2,1)} %copy.45, f32[64,6]{0,1:T(8,128)S(1)} %multiply_reduce_fusion, f32[64,6]{0,1:T(8,128)S(1)} %log_add_fusion, ...), kind=kOutput, calls=%fused_computation.28 | convolution fusion | flops 25706496 | bytes 888064 | tf_op jit(solution)/shard_map/qhk,khd->qhd/dot_general | solution.py:128
  126.0 13.1 %all-gather.8 = f32[4,64,6]{1,2,0:T(8,128)S(1)} all-gather(f32[1,64,6]{1,2,0:T(8,128)S(1)} %bitcast.177), channel_id=1, replica_groups=mesh['groups'=2,'ctx'=4,'dp'=2,'mp'=2] {'ctx'}, dimensions={0}, use_global_device_ids=true | all-gather | bytes 7680 | tf_op jit(solution)/shard_map/all_gather | solution.py:135
  139.2 18.3 %all_gather.54 = bf16[256,6,64]{2,1,0:T(8,128)(2,1)} all-gather(bf16[64,6,64]{2,1,0:T(8,128)(2,1)} %copy.55), channel_id=1, replica_groups=mesh['groups'=2,'ctx'=4,'dp'=2,'mp'=2] {'ctx'}, dimensions={0}, use_global_device_ids=true | all-gather | bytes 245760 | tf_op jit(solution)/shard_map/all_gather | solution.py:138
  159.7 1.9 %fusion.15 = bf16[64,1,6,64]{0,3,2,1:T(8,128)(2,1)} fusion(f32[256,6,64]{0,2,1:T(8,128)S(1)} %fusion.8, bf16[256,6,64]{0,2,1:T(8,128)(2,1)S(1)} %copy.59, bf16[256,1,6,64]{3,0,2,1:T(8,128)(2,1)S(1)} %all-gather.5, f32[256,6]{0,1:T(8,128)S(1)} %reshape.121, bf16[64,1,6,64]{3,2,1,0:T(8,128)(2,1)} %copy-done.2), kind=kOutput, calls=%fused_computation.27 | convolution fusion | flops 25509888 | bytes 890880 | tf_op jit(solution)/shard_map/qhk,qhd->khd/dot_general | solution.py:149
  163.1 2.1 %all-gather.6 = f32[128,768]{1,0:T(8,128)S(1)} all-gather(f32[64,768]{1,0:T(8,128)S(1)} %fusion.104), channel_id=8, replica_groups=mesh['groups'=2,'ctx'=4,'dp'=2,'mp'=2] {'mp'}, dimensions={0}, use_global_device_ids=true | all-gather | bytes 589824 | tf_op jit(solution)/shard_map/all_gather | solution.py:23
  (82 shorter events, 34.5 us)
Async XLA Ops:
  0.0 44.9 %copy-start = (bf16[384,768]{1,0:T(8,128)(2,1)S(1)}, bf16[384,768]{1,0:T(8,128)(2,1)}, u32[]{:S(2)}) copy-start(bf16[384,768]{1,0:T(8,128)(2,1)} %param.11) | copy-start | bytes 1769476
  0.0 3.4 %copy-start.5 = (bf16[1,64,768]{2,1,0:T(8,128)(2,1)S(1)}, bf16[1,64,768]{2,1,0:T(8,128)(2,1)}, u32[]{:S(2)}) copy-start(bf16[1,64,768]{2,1,0:T(8,128)(2,1)} %param.9) | copy-start | bytes 294916
  5.0 0.7 copy-start.3
  5.0 39.8 %copy-start.2 = (bf16[64,1,6,64]{3,2,1,0:T(8,128)(2,1)}, bf16[64,1,6,64]{3,2,1,0:T(8,128)(2,1)S(1)}, u32[]{:S(2)}) copy-start(bf16[64,1,6,64]{3,2,1,0:T(8,128)(2,1)S(1)} %get-tuple-element.9) | copy-start | bytes 147460
  26.1 21.1 %copy-start.1 = (f32[64,6,256]{2,0,1:T(8,128)}, f32[64,6,256]{2,0,1:T(8,128)S(1)}, u32[]{:S(2)}) copy-start(f32[64,6,256]{2,0,1:T(8,128)S(1)} %get-tuple-element.20) | copy-start | bytes 1179652
  44.9 2.4 %copy-start.7 = (bf16[64,6,64]{0,2,1:T(8,128)(2,1)}, bf16[64,6,64]{0,2,1:T(8,128)(2,1)S(1)}, u32[]{:S(2)}) copy-start(bf16[64,6,64]{0,2,1:T(8,128)(2,1)S(1)} %fusion.12) | copy-start | bytes 147460
  48.2 34.3 %collective-permute-start = (bf16[1,768]{1,0:T(2,128)(2,1)S(1)}, bf16[1,768]{1,0:T(2,128)(2,1)S(1)}, u32[]{:S(2)}, u32[]{:S(2)}) collective-permute-start(bf16[1,768]{1,0:T(2,128)(2,1)S(1)} %get-tuple-element.17), channel_id=1, source_target_pairs={{0,4},{4,8},{8,12},{1,5},{5,9},{9,13},{2,6},{6,10},{10,14},{3,7},{... | collective-permute-start | bytes 4616 | tf_op jit(solution)/shard_map/ppermute | solution.py:16
  50.9 31.6 %collective-permute-start.1 = (bf16[1,768]{1,0:T(2,128)(2,1)S(1)}, bf16[1,768]{1,0:T(2,128)(2,1)S(1)}, u32[]{:S(2)}, u32[]{:S(2)}) collective-permute-start(bf16[1,768]{1,0:T(2,128)(2,1)S(1)} %get-tuple-element.18), channel_id=1, source_target_pairs={{4,0},{8,4},{12,8},{5,1},{9,5},{13,9},{6,2},{10,6},{14,10},{7,3},{... | collective-permute-start | bytes 4616 | tf_op jit(solution)/shard_map/ppermute | solution.py:17
  88.2 0.8 copy-start.6
  92.4 7.2 %copy-start.4 = (bf16[64,1,6,64]{3,2,1,0:T(8,128)(2,1)S(1)}, bf16[64,1,6,64]{3,2,1,0:T(8,128)(2,1)}, u32[]{:S(2)}) copy-start(bf16[64,1,6,64]{3,2,1,0:T(8,128)(2,1)} %copy-done.3) | copy-start | bytes 147460
  92.4 7.2 %copy-start.9 = (pred[64]{0:T(512)(128)(4,1)S(1)}, pred[64]{0:T(512)(128)(4,1)}, u32[]{:S(2)}) copy-start(pred[64]{0:T(512)(128)(4,1)} %multiply_compare_fusion.1) | copy-start | bytes 196
  94.3 8.9 %collective-permute-start.2 = (bf16[1,1536]{1,0:T(2,128)(2,1)S(1)}, bf16[1,1536]{1,0:T(2,128)(2,1)S(1)}, u32[]{:S(2)}, u32[]{:S(2)}) collective-permute-start(bf16[1,1536]{1,0:T(2,128)(2,1)S(1)} %bitcast.178), channel_id=1, source_target_pairs={{0,4},{4,8},{8,12},{1,5},{5,9},{9,13},{2,6},{6,10},{10,14},{3,7},{... | collective-permute-start | bytes 9224 | tf_op jit(solution)/shard_map/ppermute | solution.py:16
  98.3 5.5 %collective-permute-start.3 = (bf16[1,1536]{1,0:T(2,128)(2,1)S(1)}, bf16[1,1536]{1,0:T(2,128)(2,1)S(1)}, u32[]{:S(2)}, u32[]{:S(2)}) collective-permute-start(bf16[1,1536]{1,0:T(2,128)(2,1)S(1)} %bitcast.179), channel_id=1, source_target_pairs={{4,0},{8,4},{12,8},{5,1},{9,5},{13,9},{6,2},{10,6},{14,10},{7,3},{... | collective-permute-start | bytes 9224 | tf_op jit(solution)/shard_map/ppermute | solution.py:17
  114.9 8.0 %copy-start.8 = (bf16[64,6,64]{0,2,1:T(8,128)(2,1)S(1)}, bf16[64,6,64]{0,2,1:T(8,128)(2,1)}, u32[]{:S(2)}) copy-start(bf16[64,6,64]{0,2,1:T(8,128)(2,1)} %copy-done.7) | copy-start | bytes 147460
